TPU v7x, 512 devices: a whole 4x4x16 slice. The times are simulated.
512 devices in a mesh: dp: 16 (over x, y), ctx: 32 (over z, core).
Axes of the slice: x: 4, y: 4, z: 16, core: 2. Of those that a mesh axis runs over, the one named last changes fastest.
Arguments:
- queries: bfloat16 [65536, 3072], P(('dp', 'ctx')), parts along dimension 0
- key_vectors: bfloat16 [65536, 512], P(('dp', 'ctx')), parts along dimension 0
- value_vectors: bfloat16 [65536, 512], P(('dp', 'ctx')), parts along dimension 0, may hold values from -6 to 6
- d_output: bfloat16 [65536, 3072], P(('dp', 'ctx')), parts along dimension 0, may hold values from -6 to 6
- doc_blocks: int32 [256], P('dp'), parts along dimension 0, may hold values from 1 to 4, 32 in all
Outputs:
- d_queries: bfloat16 [65536, 3072], P(('dp', 'ctx')), parts along dimension 0
- d_keys: bfloat16 [65536, 512], P(('dp', 'ctx')), parts along dimension 0
- d_values: bfloat16 [65536, 512], P(('dp', 'ctx')), parts along dimension 0
There are 16 independent parts, one for each index of `dp`. A program takes and returns all parts, laid end to end along the dimension named above; each array names one. Nothing has to cross between parts.
Inputs may be any that keep to these rules, and one draw needn't show every extreme that they name: `doc_blocks`: 16 documents that fill the pack exactly: the lengths sum to 32, and the longest is exactly 4.
All inputs are finite; a program needn't handle non-finite values.
Results may differ from a plain program's by a relative error of at most 0.011.
Values may be sent and summed in bfloat16 or wider, within the bound.
A program may use at most 64 MiB of HBM per device.

v0:
```python
import math

import jax
import jax.numpy as jnp
from jax import lax
from jax.sharding import PartitionSpec as P

QH = 24
KVH = 4
HD = 128
BLOCK = 128
SPAN = 4


def passed_along(array, axis, by):
    devices = lax.axis_size(axis)
    pairs = [(i, i + by) for i in range(devices) if 0 <= i + by < devices]
    return lax.ppermute(array, axis, pairs)


def doc_of(positions, doc_blocks):
    doc_ends = jnp.cumsum(doc_blocks) * BLOCK
    return jnp.sum((positions[:, None] >= doc_ends[None, :]).astype(jnp.int32), axis=1)


def per_device(queries, key_vectors, value_vectors, d_output, doc_blocks):
    local_rows = queries.shape[0]
    per_group = QH // KVH
    inv_root = 1.0 / math.sqrt(HD)
    key_rows = (SPAN + 1) * local_rows
    device = lax.axis_index("ctx")
    arrived = [(key_vectors, value_vectors)]
    current = (key_vectors, value_vectors)
    for distance in range(1, SPAN + 1):
        current = passed_along((current[0], current[1]), "ctx", 1)
        arrived.append(current)
    keys_all = jnp.concatenate(
        [arrived[distance][0] for distance in range(SPAN, -1, -1)], 0
    ).reshape(key_rows, KVH, HD)
    values_all = jnp.concatenate(
        [arrived[distance][1] for distance in range(SPAN, -1, -1)], 0
    ).reshape(key_rows, KVH, HD)
    query_pos = device * local_rows + jnp.arange(local_rows, dtype=jnp.int32)
    key_pos = (device - SPAN) * local_rows + jnp.arange(key_rows, dtype=jnp.int32)
    allowed = doc_of(key_pos, doc_blocks)[None, :] == doc_of(query_pos, doc_blocks)[:, None]
    allowed = allowed & (key_pos[None, :] <= query_pos[:, None]) & (key_pos[None, :] >= 0)
    queries3 = queries.reshape(local_rows, KVH, per_group, HD)
    dout3 = d_output.reshape(local_rows, KVH, per_group, HD)
    dquery_parts = []
    dkey_parts = []
    dvalue_parts = []
    for head_group in range(KVH):
        query_grp = queries3[:, head_group]
        dout_grp = dout3[:, head_group]
        key_grp = keys_all[:, head_group]
        value_grp = values_all[:, head_group]
        scores = (
            jnp.einsum("tja,ua->jtu", query_grp, key_grp, preferred_element_type=jnp.float32)
            * inv_root
        )
        scores = jnp.where(allowed[None], scores, -jnp.inf)
        top_score = jnp.max(scores, axis=-1, keepdims=True)
        probs = jnp.exp(scores - top_score)
        probs = probs / jnp.sum(probs, axis=-1, keepdims=True)
        probs_low = probs.astype(jnp.bfloat16)
        attended = jnp.einsum(
            "jtu,ua->tja", probs_low, value_grp, preferred_element_type=jnp.float32
        )
        row_delta = jnp.transpose(jnp.sum(dout_grp.astype(jnp.float32) * attended, axis=-1), (1, 0))
        dprobs = jnp.einsum("tja,ua->jtu", dout_grp, value_grp, preferred_element_type=jnp.float32)
        dscores_low = (probs * (dprobs - row_delta[..., None])).astype(jnp.bfloat16)
        dquery_parts.append(
            jnp.einsum("jtu,ua->tja", dscores_low, key_grp, preferred_element_type=jnp.float32)
            * inv_root
        )
        dkey_parts.append(
            jnp.einsum("jtu,tja->ua", dscores_low, query_grp, preferred_element_type=jnp.float32)
            * inv_root
        )
        dvalue_parts.append(
            jnp.einsum("jtu,tja->ua", probs_low, dout_grp, preferred_element_type=jnp.float32)
        )
    d_queries = jnp.stack(dquery_parts, axis=1).reshape(local_rows, QH * HD).astype(jnp.bfloat16)
    dkey_all = jnp.stack(dkey_parts, axis=1).reshape(key_rows, KVH * HD).astype(jnp.bfloat16)
    dvalue_all = jnp.stack(dvalue_parts, axis=1).reshape(key_rows, KVH * HD).astype(jnp.bfloat16)
    key_terms = [
        dkey_all[(SPAN - distance) * local_rows : (SPAN - distance + 1) * local_rows]
        for distance in range(SPAN + 1)
    ]
    value_terms = [
        dvalue_all[(SPAN - distance) * local_rows : (SPAN - distance + 1) * local_rows]
        for distance in range(SPAN + 1)
    ]
    summed_keys = key_terms[0].astype(jnp.float32)
    summed_values = value_terms[0].astype(jnp.float32)
    for distance in range(1, SPAN + 1):
        back_keys, back_values = passed_along(
            (key_terms[distance], value_terms[distance]), "ctx", -distance
        )
        summed_keys = summed_keys + back_keys.astype(jnp.float32)
        summed_values = summed_values + back_values.astype(jnp.float32)
    return (d_queries, summed_keys.astype(jnp.bfloat16), summed_values.astype(jnp.bfloat16))


def solution(mesh):
    in_specs = (
        P(("dp", "ctx"), None),
        P(("dp", "ctx"), None),
        P(("dp", "ctx"), None),
        P(("dp", "ctx"), None),
        P("dp"),
    )
    out_specs = (P(("dp", "ctx"), None), P(("dp", "ctx"), None), P(("dp", "ctx"), None))
    return jax.shard_map(
        per_device, mesh=mesh, in_specs=in_specs, out_specs=out_specs, check_vma=False
    )
```

profile of v0, /device:TPU:198, one launch (start us, length us, event | category | flops | bytes accessed | tf_op | source)
XLA Modules:
  0.0 107.2 jit_solution(1872677491408735854)
XLA Ops:
  1.8 1.9 %collective-permute-start.4 = (bf16[128,512]{0,1:T(8,128)(2,1)S(1)}, bf16[128,512]{0,1:T(8,128)(2,1)S(1)}, u32[]{:S(2)}, u32[]{:S(2)}) collective-permute-start(bf16[128,512]{0,1:T(8,128)(2,1)S(1)} %copy.132), channel_id=1, source_target_pairs={{0,1},{1,2},{2,3},{3,4},{4,5},{5,6},{6,7},{7,8},{8,9},{9,10},{10,1... | collective-permute-start | bytes 393224 | tf_op jit(solution)/shard_map/ppermute | solution.py:18
  4.7 3.9 %collective-permute-start = (bf16[128,512]{0,1:T(8,128)(2,1)S(1)}, bf16[128,512]{0,1:T(8,128)(2,1)S(1)}, u32[]{:S(2)}, u32[]{:S(2)}) collective-permute-start(bf16[128,512]{0,1:T(8,128)(2,1)S(1)} %copy.126), channel_id=1, source_target_pairs={{0,1},{1,2},{2,3},{3,4},{4,5},{5,6},{6,7},{7,8},{8,9},{9,10},{10,1... | collective-permute-start | bytes 393224 | tf_op jit(solution)/shard_map/ppermute | solution.py:18
  11.0 1.9 %collective-permute-start.1 = (bf16[128,512]{0,1:T(8,128)(2,1)S(1)}, bf16[128,512]{0,1:T(8,128)(2,1)S(1)}, u32[]{:S(2)}, u32[]{:S(2)}) collective-permute-start(bf16[128,512]{0,1:T(8,128)(2,1)S(1)} %collective-permute-done), channel_id=1, source_target_pairs={{0,1},{1,2},{2,3},{3,4},{4,5},{5,6},{6,7},{7,8},{8,9},{9,10},{10,1... | collective-permute-start | bytes 393224 | tf_op jit(solution)/shard_map/ppermute | solution.py:18
  13.0 4.6 %collective-permute-start.5 = (bf16[128,512]{0,1:T(8,128)(2,1)S(1)}, bf16[128,512]{0,1:T(8,128)(2,1)S(1)}, u32[]{:S(2)}, u32[]{:S(2)}) collective-permute-start(bf16[128,512]{0,1:T(8,128)(2,1)S(1)} %collective-permute-done.4), channel_id=1, source_target_pairs={{0,1},{1,2},{2,3},{3,4},{4,5},{5,6},{6,7},{7,8},{8,9},{9,10},{10,1... | collective-permute-start | bytes 393224 | tf_op jit(solution)/shard_map/ppermute | solution.py:18
  17.7 2.0 %collective-permute-start.2 = (bf16[128,512]{0,1:T(8,128)(2,1)S(1)}, bf16[128,512]{0,1:T(8,128)(2,1)S(1)}, u32[]{:S(2)}, u32[]{:S(2)}) collective-permute-start(bf16[128,512]{0,1:T(8,128)(2,1)S(1)} %collective-permute-done.1), channel_id=1, source_target_pairs={{0,1},{1,2},{2,3},{3,4},{4,5},{5,6},{6,7},{7,8},{8,9},{9,10},{10,1... | collective-permute-start | bytes 393224 | tf_op jit(solution)/shard_map/ppermute | solution.py:18
  24.2 5.6 %collective-permute-start.6 = (bf16[128,512]{0,1:T(8,128)(2,1)S(1)}, bf16[128,512]{0,1:T(8,128)(2,1)S(1)}, u32[]{:S(2)}, u32[]{:S(2)}) collective-permute-start(bf16[128,512]{0,1:T(8,128)(2,1)S(1)} %collective-permute-done.5), channel_id=1, source_target_pairs={{0,1},{1,2},{2,3},{3,4},{4,5},{5,6},{6,7},{7,8},{8,9},{9,10},{10,1... | collective-permute-start | bytes 393224 | tf_op jit(solution)/shard_map/ppermute | solution.py:18
  29.8 1.9 %collective-permute-start.3 = (bf16[128,512]{0,1:T(8,128)(2,1)S(1)}, bf16[128,512]{0,1:T(8,128)(2,1)S(1)}, u32[]{:S(2)}, u32[]{:S(2)}) collective-permute-start(bf16[128,512]{0,1:T(8,128)(2,1)S(1)} %collective-permute-done.2), channel_id=1, source_target_pairs={{0,1},{1,2},{2,3},{3,4},{4,5},{5,6},{6,7},{7,8},{8,9},{9,10},{10,1... | collective-permute-start | bytes 393224 | tf_op jit(solution)/shard_map/ppermute | solution.py:18
  32.1 5.4 %collective-permute-start.7 = (bf16[128,512]{0,1:T(8,128)(2,1)S(1)}, bf16[128,512]{0,1:T(8,128)(2,1)S(1)}, u32[]{:S(2)}, u32[]{:S(2)}) collective-permute-start(bf16[128,512]{0,1:T(8,128)(2,1)S(1)} %collective-permute-done.6), channel_id=1, source_target_pairs={{0,1},{1,2},{2,3},{3,4},{4,5},{5,6},{6,7},{7,8},{8,9},{9,10},{10,1... | collective-permute-start | bytes 393224 | tf_op jit(solution)/shard_map/ppermute | solution.py:18
  39.5 1.7 %fusion.109 = (f32[6,128]{1,0:T(8,128)S(1)}, f32[6,128,640]{1,2,0:T(8,128)S(1)}) fusion(pred[128,640]{0,1:T(8,128)(4,1)S(1)} %and_and_fusion, bf16[128,4,6,128]{0,3,2,1:T(8,128)(2,1)} %bitcast.398, bf16[640,4,128]{0,2,1:T(8,128)(2,1)S(1)} %bitcast.382), kind=kOutput, calls=%fused_computation.173 | convolution fusion | flops 127795840 | bytes 2411520 | tf_op jit(solution)/shard_map/sub | solution.py:63
  43.6 2.0 %fusion.50 = bf16[640,1,128]{0,2,1:T(8,128)(2,1)} fusion(bf16[6,128,640]{1,2,0:T(8,128)(2,1)S(1)} %fusion.9, bf16[128,4,6,128]{0,3,2,1:T(8,128)(2,1)} %bitcast.399), kind=kOutput, calls=%fused_computation.78 | convolution fusion | flops 125992960 | bytes 1343488 | tf_op jit(solution)/shard_map/jtu,tja->ua/dot_general | solution.py:77
  50.8 2.0 %fusion.51 = bf16[640,1,128]{0,2,1:T(8,128)(2,1)} fusion(bf16[6,128,640]{1,2,0:T(8,128)(2,1)S(1)} %fusion.11, bf16[128,4,6,128]{0,3,2,1:T(8,128)(2,1)} %bitcast.401), kind=kOutput, calls=%fused_computation.79 | convolution fusion | flops 125992960 | bytes 1343488 | tf_op jit(solution)/shard_map/jtu,tja->ua/dot_general | solution.py:77
  53.9 1.7 %fusion.107 = (f32[6,128]{1,0:T(8,128)S(1)}, f32[6,128,640]{1,2,0:T(8,128)S(1)}) fusion(pred[128,640]{0,1:T(8,128)(4,1)S(1)} %and_and_fusion, bf16[128,4,6,128]{0,3,2,1:T(8,128)(2,1)} %bitcast.402, bf16[640,4,128]{0,2,1:T(8,128)(2,1)S(1)} %bitcast.386), kind=kOutput, calls=%fused_computation.171 | convolution fusion | flops 127795840 | bytes 2411520 | tf_op jit(solution)/shard_map/sub | solution.py:63
  58.0 2.0 %fusion.48 = bf16[640,1,128]{0,2,1:T(8,128)(2,1)} fusion(bf16[6,128,640]{1,2,0:T(8,128)(2,1)S(1)} %fusion.5, bf16[128,4,6,128]{0,3,2,1:T(8,128)(2,1)} %bitcast.403), kind=kOutput, calls=%fused_computation.76 | convolution fusion | flops 125992960 | bytes 1343488 | tf_op jit(solution)/shard_map/jtu,tja->ua/dot_general | solution.py:77
  61.0 1.7 %fusion.108 = (f32[6,128]{1,0:T(8,128)S(1)}, f32[6,128,640]{1,2,0:T(8,128)S(1)}) fusion(pred[128,640]{0,1:T(8,128)(4,1)S(1)} %and_and_fusion, bf16[128,4,6,128]{0,3,2,1:T(8,128)(2,1)} %bitcast.404, bf16[640,4,128]{0,2,1:T(8,128)(2,1)S(1)} %bitcast.388), kind=kOutput, calls=%fused_computation.172 | convolution fusion | flops 127795840 | bytes 2411520 | tf_op jit(solution)/shard_map/sub | solution.py:63
  70.4 1.9 %collective-permute-start.9 = (bf16[128,512]{1,0:T(8,128)(2,1)S(1)}, bf16[128,512]{1,0:T(8,128)(2,1)S(1)}, u32[]{:S(2)}, u32[]{:S(2)}) collective-permute-start(bf16[128,512]{1,0:T(8,128)(2,1)S(1)} %copy.179), channel_id=1, source_target_pairs={{2,0},{3,1},{4,2},{5,3},{6,4},{7,5},{8,6},{9,7},{10,8},{11,9},{12,... | collective-permute-start | bytes 393224 | tf_op jit(solution)/shard_map/ppermute | solution.py:18
  72.4 4.8 %collective-permute-start.13 = (bf16[128,512]{1,0:T(8,128)(2,1)S(1)}, bf16[128,512]{1,0:T(8,128)(2,1)S(1)}, u32[]{:S(2)}, u32[]{:S(2)}) collective-permute-start(bf16[128,512]{1,0:T(8,128)(2,1)S(1)} %copy.192), channel_id=1, source_target_pairs={{2,0},{3,1},{4,2},{5,3},{6,4},{7,5},{8,6},{9,7},{10,8},{11,9},{12,... | collective-permute-start | bytes 393224 | tf_op jit(solution)/shard_map/ppermute | solution.py:18
  77.2 1.9 %collective-permute-start.14 = (bf16[128,512]{1,0:T(8,128)(2,1)S(1)}, bf16[128,512]{1,0:T(8,128)(2,1)S(1)}, u32[]{:S(2)}, u32[]{:S(2)}) collective-permute-start(bf16[128,512]{1,0:T(8,128)(2,1)S(1)} %copy.193), channel_id=1, source_target_pairs={{3,0},{4,1},{5,2},{6,3},{7,4},{8,5},{9,6},{10,7},{11,8},{12,9},{13... | collective-permute-start | bytes 393224 | tf_op jit(solution)/shard_map/ppermute | solution.py:18
  79.1 1.9 %collective-permute-start.15 = (bf16[128,512]{1,0:T(8,128)(2,1)S(1)}, bf16[128,512]{1,0:T(8,128)(2,1)S(1)}, u32[]{:S(2)}, u32[]{:S(2)}) collective-permute-start(bf16[128,512]{1,0:T(8,128)(2,1)S(1)} %copy.194), channel_id=1, source_target_pairs={{4,0},{5,1},{6,2},{7,3},{8,4},{9,5},{10,6},{11,7},{12,8},{13,9},{1... | collective-permute-start | bytes 393224 | tf_op jit(solution)/shard_map/ppermute | solution.py:18
  81.0 1.9 %collective-permute-start.12 = (bf16[128,512]{1,0:T(8,128)(2,1)S(1)}, bf16[128,512]{1,0:T(8,128)(2,1)S(1)}, u32[]{:S(2)}, u32[]{:S(2)}) collective-permute-start(bf16[128,512]{1,0:T(8,128)(2,1)S(1)} %copy.190), channel_id=1, source_target_pairs={{1,0},{2,1},{3,2},{4,3},{5,4},{6,5},{7,6},{8,7},{9,8},{10,9},{11,1... | collective-permute-start | bytes 393224 | tf_op jit(solution)/shard_map/ppermute | solution.py:18
  83.3 1.9 %collective-permute-start.10 = (bf16[128,512]{1,0:T(8,128)(2,1)S(1)}, bf16[128,512]{1,0:T(8,128)(2,1)S(1)}, u32[]{:S(2)}, u32[]{:S(2)}) collective-permute-start(bf16[128,512]{1,0:T(8,128)(2,1)S(1)} %copy.180), channel_id=1, source_target_pairs={{3,0},{4,1},{5,2},{6,3},{7,4},{8,5},{9,6},{10,7},{11,8},{12,9},{13... | collective-permute-start | bytes 393224 | tf_op jit(solution)/shard_map/ppermute | solution.py:18
  85.8 1.9 %collective-permute-start.11 = (bf16[128,512]{1,0:T(8,128)(2,1)S(1)}, bf16[128,512]{1,0:T(8,128)(2,1)S(1)}, u32[]{:S(2)}, u32[]{:S(2)}) collective-permute-start(bf16[128,512]{1,0:T(8,128)(2,1)S(1)} %copy.181), channel_id=1, source_target_pairs={{4,0},{5,1},{6,2},{7,3},{8,4},{9,5},{10,6},{11,7},{12,8},{13,9},{1... | collective-permute-start | bytes 393224 | tf_op jit(solution)/shard_map/ppermute | solution.py:18
  87.7 8.1 %collective-permute-done.15 = bf16[128,512]{1,0:T(8,128)(2,1)S(1)} collective-permute-done((bf16[128,512]{1,0:T(8,128)(2,1)S(1)}, bf16[128,512]{1,0:T(8,128)(2,1)S(1)}, u32[]{:S(2)}, u32[]{:S(2)}) %collective-permute-start.15) | collective-permute-done | bytes 131104 | tf_op jit(solution)/shard_map/ppermute | solution.py:18
  95.9 1.9 %collective-permute-start.8 = (bf16[128,512]{1,0:T(8,128)(2,1)S(1)}, bf16[128,512]{1,0:T(8,128)(2,1)S(1)}, u32[]{:S(2)}, u32[]{:S(2)}) collective-permute-start(bf16[128,512]{1,0:T(8,128)(2,1)S(1)} %copy.177), channel_id=1, source_target_pairs={{1,0},{2,1},{3,2},{4,3},{5,4},{6,5},{7,6},{8,7},{9,8},{10,9},{11,1... | collective-permute-start | bytes 393224 | tf_op jit(solution)/shard_map/ppermute | solution.py:18
  98.5 7.9 %collective-permute-done.11 = bf16[128,512]{1,0:T(8,128)(2,1)S(1)} collective-permute-done((bf16[128,512]{1,0:T(8,128)(2,1)S(1)}, bf16[128,512]{1,0:T(8,128)(2,1)S(1)}, u32[]{:S(2)}, u32[]{:S(2)}) %collective-permute-start.11) | collective-permute-done | bytes 131104 | tf_op jit(solution)/shard_map/ppermute | solution.py:18
  (126 shorter events, 32.9 us)
Async XLA Ops:
  0.6 9.6 %copy-start.20 = (s32[16]{0:T(128)S(1)}, s32[16]{0:T(128)}, u32[]{:S(2)}) copy-start(s32[16]{0:T(128)} %param.9) | copy-start | bytes 196
  0.6 19.0 %copy-start.5 = (bf16[128,3072]{1,0:T(8,128)(2,1)S(1)}, bf16[128,3072]{1,0:T(8,128)(2,1)}, u32[]{:S(2)}) copy-start(bf16[128,3072]{1,0:T(8,128)(2,1)} %param.5) | copy-start | bytes 2359300
  1.8 11.3 %collective-permute-start.4 = (bf16[128,512]{0,1:T(8,128)(2,1)S(1)}, bf16[128,512]{0,1:T(8,128)(2,1)S(1)}, u32[]{:S(2)}, u32[]{:S(2)}) collective-permute-start(bf16[128,512]{0,1:T(8,128)(2,1)S(1)} %copy.132), channel_id=1, source_target_pairs={{0,1},{1,2},{2,3},{3,4},{4,5},{5,6},{6,7},{7,8},{8,9},{9,10},{10,1... | collective-permute-start | bytes 393224 | tf_op jit(solution)/shard_map/ppermute | solution.py:18
  4.7 6.3 %collective-permute-start = (bf16[128,512]{0,1:T(8,128)(2,1)S(1)}, bf16[128,512]{0,1:T(8,128)(2,1)S(1)}, u32[]{:S(2)}, u32[]{:S(2)}) collective-permute-start(bf16[128,512]{0,1:T(8,128)(2,1)S(1)} %copy.126), channel_id=1, source_target_pairs={{0,1},{1,2},{2,3},{3,4},{4,5},{5,6},{6,7},{7,8},{8,9},{9,10},{10,1... | collective-permute-start | bytes 393224 | tf_op jit(solution)/shard_map/ppermute | solution.py:18
  11.0 6.7 %collective-permute-start.1 = (bf16[128,512]{0,1:T(8,128)(2,1)S(1)}, bf16[128,512]{0,1:T(8,128)(2,1)S(1)}, u32[]{:S(2)}, u32[]{:S(2)}) collective-permute-start(bf16[128,512]{0,1:T(8,128)(2,1)S(1)} %collective-permute-done), channel_id=1, source_target_pairs={{0,1},{1,2},{2,3},{3,4},{4,5},{5,6},{6,7},{7,8},{8,9},{9,10},{10,1... | collective-permute-start | bytes 393224 | tf_op jit(solution)/shard_map/ppermute | solution.py:18
  13.0 11.2 %collective-permute-start.5 = (bf16[128,512]{0,1:T(8,128)(2,1)S(1)}, bf16[128,512]{0,1:T(8,128)(2,1)S(1)}, u32[]{:S(2)}, u32[]{:S(2)}) collective-permute-start(bf16[128,512]{0,1:T(8,128)(2,1)S(1)} %collective-permute-done.4), channel_id=1, source_target_pairs={{0,1},{1,2},{2,3},{3,4},{4,5},{5,6},{6,7},{7,8},{8,9},{9,10},{10,1... | collective-permute-start | bytes 393224 | tf_op jit(solution)/shard_map/ppermute | solution.py:18
  17.7 12.1 %collective-permute-start.2 = (bf16[128,512]{0,1:T(8,128)(2,1)S(1)}, bf16[128,512]{0,1:T(8,128)(2,1)S(1)}, u32[]{:S(2)}, u32[]{:S(2)}) collective-permute-start(bf16[128,512]{0,1:T(8,128)(2,1)S(1)} %collective-permute-done.1), channel_id=1, source_target_pairs={{0,1},{1,2},{2,3},{3,4},{4,5},{5,6},{6,7},{7,8},{8,9},{9,10},{10,1... | collective-permute-start | bytes 393224 | tf_op jit(solution)/shard_map/ppermute | solution.py:18
  24.2 7.8 %collective-permute-start.6 = (bf16[128,512]{0,1:T(8,128)(2,1)S(1)}, bf16[128,512]{0,1:T(8,128)(2,1)S(1)}, u32[]{:S(2)}, u32[]{:S(2)}) collective-permute-start(bf16[128,512]{0,1:T(8,128)(2,1)S(1)} %collective-permute-done.5), channel_id=1, source_target_pairs={{0,1},{1,2},{2,3},{3,4},{4,5},{5,6},{6,7},{7,8},{8,9},{9,10},{10,1... | collective-permute-start | bytes 393224 | tf_op jit(solution)/shard_map/ppermute | solution.py:18
  29.8 7.7 %collective-permute-start.3 = (bf16[128,512]{0,1:T(8,128)(2,1)S(1)}, bf16[128,512]{0,1:T(8,128)(2,1)S(1)}, u32[]{:S(2)}, u32[]{:S(2)}) collective-permute-start(bf16[128,512]{0,1:T(8,128)(2,1)S(1)} %collective-permute-done.2), channel_id=1, source_target_pairs={{0,1},{1,2},{2,3},{3,4},{4,5},{5,6},{6,7},{7,8},{8,9},{9,10},{10,1... | collective-permute-start | bytes 393224 | tf_op jit(solution)/shard_map/ppermute | solution.py:18
  32.1 6.4 %collective-permute-start.7 = (bf16[128,512]{0,1:T(8,128)(2,1)S(1)}, bf16[128,512]{0,1:T(8,128)(2,1)S(1)}, u32[]{:S(2)}, u32[]{:S(2)}) collective-permute-start(bf16[128,512]{0,1:T(8,128)(2,1)S(1)} %collective-permute-done.6), channel_id=1, source_target_pairs={{0,1},{1,2},{2,3},{3,4},{4,5},{5,6},{6,7},{7,8},{8,9},{9,10},{10,1... | collective-permute-start | bytes 393224 | tf_op jit(solution)/shard_map/ppermute | solution.py:18
  65.1 1.8 %copy-start.6 = (bf16[128,1,6,128]{0,3,2,1:T(8,128)(2,1)S(1)}, bf16[128,1,6,128]{0,3,2,1:T(8,128)(2,1)}, u32[]{:S(2)}) copy-start(bf16[128,1,6,128]{0,3,2,1:T(8,128)(2,1)} %fusion.42) | copy-start | bytes 589828
  65.1 1.8 %copy-start.7 = (bf16[128,1,6,128]{0,3,2,1:T(8,128)(2,1)S(1)}, bf16[128,1,6,128]{0,3,2,1:T(8,128)(2,1)}, u32[]{:S(2)}) copy-start(bf16[128,1,6,128]{0,3,2,1:T(8,128)(2,1)} %fusion.43) | copy-start | bytes 589828
  65.2 1.8 %copy-start.8 = (bf16[128,1,6,128]{0,3,2,1:T(8,128)(2,1)S(1)}, bf16[128,1,6,128]{0,3,2,1:T(8,128)(2,1)}, u32[]{:S(2)}) copy-start(bf16[128,1,6,128]{0,3,2,1:T(8,128)(2,1)} %fusion.40) | copy-start | bytes 589828
  66.6 1.7 %copy-start.17 = (bf16[640,1,128]{0,2,1:T(8,128)(2,1)S(1)}, bf16[640,1,128]{0,2,1:T(8,128)(2,1)}, u32[]{:S(2)}) copy-start(bf16[640,1,128]{0,2,1:T(8,128)(2,1)} %fusion.50) | copy-start | bytes 491524
  66.6 1.7 %copy-start.18 = (bf16[640,1,128]{0,2,1:T(8,128)(2,1)S(1)}, bf16[640,1,128]{0,2,1:T(8,128)(2,1)}, u32[]{:S(2)}) copy-start(bf16[640,1,128]{0,2,1:T(8,128)(2,1)} %fusion.51) | copy-start | bytes 491524
  66.6 1.7 %copy-start.19 = (bf16[640,1,128]{0,2,1:T(8,128)(2,1)S(1)}, bf16[640,1,128]{0,2,1:T(8,128)(2,1)}, u32[]{:S(2)}) copy-start(bf16[640,1,128]{0,2,1:T(8,128)(2,1)} %fusion.48) | copy-start | bytes 491524
  70.4 28.1 %collective-permute-start.9 = (bf16[128,512]{1,0:T(8,128)(2,1)S(1)}, bf16[128,512]{1,0:T(8,128)(2,1)S(1)}, u32[]{:S(2)}, u32[]{:S(2)}) collective-permute-start(bf16[128,512]{1,0:T(8,128)(2,1)S(1)} %copy.179), channel_id=1, source_target_pairs={{2,0},{3,1},{4,2},{5,3},{6,4},{7,5},{8,6},{9,7},{10,8},{11,9},{12,... | collective-permute-start | bytes 393224 | tf_op jit(solution)/shard_map/ppermute | solution.py:18
  72.4 10.9 %collective-permute-start.13 = (bf16[128,512]{1,0:T(8,128)(2,1)S(1)}, bf16[128,512]{1,0:T(8,128)(2,1)S(1)}, u32[]{:S(2)}, u32[]{:S(2)}) collective-permute-start(bf16[128,512]{1,0:T(8,128)(2,1)S(1)} %copy.192), channel_id=1, source_target_pairs={{2,0},{3,1},{4,2},{5,3},{6,4},{7,5},{8,6},{9,7},{10,8},{11,9},{12,... | collective-permute-start | bytes 393224 | tf_op jit(solution)/shard_map/ppermute | solution.py:18
  77.2 8.6 %collective-permute-start.14 = (bf16[128,512]{1,0:T(8,128)(2,1)S(1)}, bf16[128,512]{1,0:T(8,128)(2,1)S(1)}, u32[]{:S(2)}, u32[]{:S(2)}) collective-permute-start(bf16[128,512]{1,0:T(8,128)(2,1)S(1)} %copy.193), channel_id=1, source_target_pairs={{3,0},{4,1},{5,2},{6,3},{7,4},{8,5},{9,6},{10,7},{11,8},{12,9},{13... | collective-permute-start | bytes 393224 | tf_op jit(solution)/shard_map/ppermute | solution.py:18
  79.1 16.8 %collective-permute-start.15 = (bf16[128,512]{1,0:T(8,128)(2,1)S(1)}, bf16[128,512]{1,0:T(8,128)(2,1)S(1)}, u32[]{:S(2)}, u32[]{:S(2)}) collective-permute-start(bf16[128,512]{1,0:T(8,128)(2,1)S(1)} %copy.194), channel_id=1, source_target_pairs={{4,0},{5,1},{6,2},{7,3},{8,4},{9,5},{10,6},{11,7},{12,8},{13,9},{1... | collective-permute-start | bytes 393224 | tf_op jit(solution)/shard_map/ppermute | solution.py:18
  81.0 16.8 %collective-permute-start.12 = (bf16[128,512]{1,0:T(8,128)(2,1)S(1)}, bf16[128,512]{1,0:T(8,128)(2,1)S(1)}, u32[]{:S(2)}, u32[]{:S(2)}) collective-permute-start(bf16[128,512]{1,0:T(8,128)(2,1)S(1)} %copy.190), channel_id=1, source_target_pairs={{1,0},{2,1},{3,2},{4,3},{5,4},{6,5},{7,6},{8,7},{9,8},{10,9},{11,1... | collective-permute-start | bytes 393224 | tf_op jit(solution)/shard_map/ppermute | solution.py:18
  83.3 15.2 %collective-permute-start.10 = (bf16[128,512]{1,0:T(8,128)(2,1)S(1)}, bf16[128,512]{1,0:T(8,128)(2,1)S(1)}, u32[]{:S(2)}, u32[]{:S(2)}) collective-permute-start(bf16[128,512]{1,0:T(8,128)(2,1)S(1)} %copy.180), channel_id=1, source_target_pairs={{3,0},{4,1},{5,2},{6,3},{7,4},{8,5},{9,6},{10,7},{11,8},{12,9},{13... | collective-permute-start | bytes 393224 | tf_op jit(solution)/shard_map/ppermute | solution.py:18
  85.8 20.6 %collective-permute-start.11 = (bf16[128,512]{1,0:T(8,128)(2,1)S(1)}, bf16[128,512]{1,0:T(8,128)(2,1)S(1)}, u32[]{:S(2)}, u32[]{:S(2)}) collective-permute-start(bf16[128,512]{1,0:T(8,128)(2,1)S(1)} %copy.181), channel_id=1, source_target_pairs={{4,0},{5,1},{6,2},{7,3},{8,4},{9,5},{10,6},{11,7},{12,8},{13,9},{1... | collective-permute-start | bytes 393224 | tf_op jit(solution)/shard_map/ppermute | solution.py:18
  95.9 10.6 %collective-permute-start.8 = (bf16[128,512]{1,0:T(8,128)(2,1)S(1)}, bf16[128,512]{1,0:T(8,128)(2,1)S(1)}, u32[]{:S(2)}, u32[]{:S(2)}) collective-permute-start(bf16[128,512]{1,0:T(8,128)(2,1)S(1)} %copy.177), channel_id=1, source_target_pairs={{1,0},{2,1},{3,2},{4,3},{5,4},{6,5},{7,6},{8,7},{9,8},{10,9},{11,1... | collective-permute-start | bytes 393224 | tf_op jit(solution)/shard_map/ppermute | solution.py:18
  (13 other events, 15.5 us)
where the time goes:
time: 108 us; the launch traced here: 107 us
  starting transfers between devices  45.5 us (42%)
  matrix products  26.6 us (25%)
  waiting for transfers between devices  17.9 us (17%)
  local copies, waits for them, and re-layouts  12.7 us (12%)
  other arithmetic  3.14 us (3%)
  between operations  1.39 us (1%)
    ppermute x16, starting transfers between devices, passed_along(): return lax.ppermute(array, axis, pairs)  45.5 us
    ppermute x16, waiting for transfers between devices, passed_along(): return lax.ppermute(array, axis, pairs)  17.9 us
    unnamed x59, local copies, waits for them, and re-layouts  11 us
    dot_general x4, matrix products, per_device(): jnp.einsum('jtu,tja->ua', dscores_low, query_grp, preferred_element_type=...  7.56 us
    sub x4, matrix products, per_device(): probs = jnp.exp(scores - top_score)  6.87 us
    dot_general x4, matrix products, per_device(): jnp.einsum('jtu,tja->ua', probs_low, dout_grp, preferred_element_type=jnp...  4.51 us
    dot_general x4, matrix products, per_device(): jnp.einsum('jtu,ua->tja', dscores_low, key_grp, preferred_element_type=jn...  3.38 us
    dot_general x4, matrix products, per_device(): jnp.einsum('jtu,ua->tja', probs_low, value_grp, preferred_element_type=jn...  2.35 us
  transfers between devices with their start and end apart: 16, of which 5 were waited for; matrix products, arithmetic and copies ran while one was open for 8% of the time, Pallas kernels for 0%

commit v1 on v0

v1 whole, which is shorter than its diff:
```python
import functools
import math

import jax
import jax.numpy as jnp
from jax import lax
from jax.experimental import pallas as pl
from jax.experimental.pallas import tpu as pltpu
from jax.sharding import PartitionSpec as P

QH = 24
KVH = 4
HD = 128
PER = QH // KVH
ROWS = 128
SPAN = 4
NDOCS = 16
WIDE = PER * HD
PAIRS = PER // 2
INV_ROOT = 1.0 / math.sqrt(HD)
EXP2_SCALE = INV_ROOT * math.log2(math.e)
MESH = pl.DeviceIdType.MESH
NT = (((1,), (1,)), ((), ()))
NN = (((1,), (0,)), ((), ()))
KEYS = SPAN * ROWS


def dot(a, b, dims):
    return lax.dot_general(a, b, dims, preferred_element_type=jnp.float32)


def kernel(
    n_ctx,
    docs,
    q_hbm,
    k_hbm,
    v_hbm,
    do_hbm,
    dq_hbm,
    dk_out,
    dv_out,
    q_v,
    do_v,
    dq_v,
    kv,
    k_t,
    p_s,
    ds_s,
    terms,
    own_terms,
    sums,
    back,
    load_sem,
    kv_sem,
    store_sem,
    send_sem,
    recv_sem,
    back_send,
    back_recv,
):
    me = lax.axis_index("ctx")
    core = lax.rem(me, 2)
    chip = lax.div(me, 2)
    chips = n_ctx // 2
    nxt = lax.rem(chip + 1, chips) * 2
    prv = lax.rem(chip + chips - 1, chips) * 2
    sibling = chip * 2 + (1 - core)
    cross_next = nxt + (1 - core)
    cross_prev = prv + (1 - core)
    is_even = core == 0

    def kv_load(g, which):
        src = (k_hbm, v_hbm)[which]
        return pltpu.make_async_copy(
            src.at[:, g * HD : (g + 1) * HD], kv.at[g, which, 0:ROWS], kv_sem.at[g, which]
        )

    for g in range(KVH):
        for which in range(2):
            kv_load(g, which).start()

    def q_load(g):
        cols = slice(g * WIDE, (g + 1) * WIDE)
        return (
            pltpu.make_async_copy(q_hbm.at[:, cols], q_v.at[g], load_sem.at[g, 0]),
            pltpu.make_async_copy(do_hbm.at[:, cols], do_v.at[g], load_sem.at[g, 1]),
        )

    for g in range(KVH):
        for copy in q_load(g):
            copy.start()

    barrier = pltpu.get_barrier_semaphore()

    def greet(device):
        pl.semaphore_signal(barrier, inc=1, device_id={"ctx": device}, device_id_type=MESH)

    greet(sibling)
    greet(cross_next)
    greet(cross_prev)

    @pl.when(is_even)
    def _():
        greet(nxt)
        greet(prv)

    end = jnp.int32(0)
    start = jnp.int32(0)
    for i in range(NDOCS):
        end = end + docs[i]
        start = jnp.where(end <= me, end, start)
    inside = [me - d >= start for d in range(SPAN)]

    for g in range(KVH):
        for which in range(2):
            kv_load(g, which).wait()

    @pl.when(is_even)
    def _():
        pl.semaphore_wait(barrier, 5)

    @pl.when(core == 1)
    def _():
        pl.semaphore_wait(barrier, 3)

    def kv_copy(g, from_slot, to_slot, kind, device):
        return pltpu.make_async_remote_copy(
            src_ref=kv.at[g, :, pl.ds(pl.multiple_of(from_slot * ROWS, ROWS), ROWS)],
            dst_ref=kv.at[g, :, pl.ds(pl.multiple_of(to_slot * ROWS, ROWS), ROWS)],
            send_sem=send_sem.at[kind, g],
            recv_sem=recv_sem.at[to_slot, g],
            device_id={"ctx": device},
            device_id_type=MESH,
        )

    cross_slot = 3 - 2 * core
    relay_slot = 1 + 2 * core

    def own_cross(g):
        return kv_copy(g, 0, cross_slot, 0, cross_next)

    def own_sibling(g):
        return kv_copy(g, 0, 1, 1, sibling)

    def relay_sibling(g):
        return kv_copy(g, relay_slot, 2, 2, sibling)

    def relay_cross(g):
        return kv_copy(g, 1, 3, 3, nxt)

    def send_own(g):
        own_cross(g).start()

        @pl.when(is_even)
        def _():
            own_sibling(g).start()

    def wait_slot(g, slot):
        kv_copy(g, 0, slot, 0, sibling).wait_recv()

    def relay(g):
        wait_slot(g, relay_slot)
        relay_sibling(g).start()

        @pl.when(is_even)
        def _():
            relay_cross(g).start()

    def back_copy(src, slot, kind, g, device):
        return pltpu.make_async_remote_copy(
            src_ref=src,
            dst_ref=back.at[slot, g],
            send_sem=back_send.at[kind, g],
            recv_sem=back_recv.at[slot, g],
            device_id={"ctx": device},
            device_id_type=MESH,
        )

    far = 3 - 2 * core
    far_device = jnp.where(is_even, prv, sibling)

    def send_near(g):
        return back_copy(terms.at[g, 1], 0, 0, g, sibling)

    def send_far(g):
        return back_copy(terms.at[g, far - 1], 3 - core, 1, g, far_device)

    def send_sum(g):
        return back_copy(sums.at[g], 1, 2, g, cross_prev)

    def wait_back(slot, g):
        back_copy(sums.at[g], slot, 2, g, sibling).wait_recv()

    def reduce(g):
        wait_back(0, g)

        @pl.when(is_even)
        def _():
            wait_back(3, g)
            for w in range(2):
                total = terms[g, 0, w].astype(jnp.float32) + back[0, g, w].astype(jnp.float32)
                sums[g, w] = (total + back[3, g, w].astype(jnp.float32)).astype(jnp.bfloat16)

        @pl.when(core == 1)
        def _():
            for w in range(2):
                total = terms[g, 2, w].astype(jnp.float32) + back[0, g, w].astype(jnp.float32)
                sums[g, w] = total.astype(jnp.bfloat16)

        send_sum(g).start()

    def finish(g):
        wait_back(1, g)

        @pl.when(is_even)
        def _():
            wait_back(2, g)
            for w in range(2):
                own_terms[g, w] += back[2, g, w].astype(jnp.float32)

        for w in range(2):
            own_terms[g, w] += back[1, g, w].astype(jnp.float32)

    later = lax.broadcasted_iota(jnp.int32, (ROWS, 2 * ROWS), 0) > lax.rem(
        lax.broadcasted_iota(jnp.int32, (ROWS, 2 * ROWS), 1), ROWS
    )

    def compute(g):
        for which in range(2):
            pltpu.make_async_copy(
                (q_v, do_v)[which].at[g], (q_v, do_v)[which].at[g], load_sem.at[g, which]
            ).wait()
        keys = kv[g, 0]
        k_t[...] = keys.T
        for pair in range(PAIRS):
            lo = pair * 2 * HD
            q2 = jnp.concatenate([q_v[g, :, lo : lo + HD], q_v[g, :, lo + HD : lo + 2 * HD]], 0)
            do2 = jnp.concatenate([do_v[g, :, lo : lo + HD], do_v[g, :, lo + HD : lo + 2 * HD]], 0)
            blocks = []
            tops = []
            for d in range(SPAN):
                k_d = kv[g, 0, d * ROWS : (d + 1) * ROWS]
                if d > 0:
                    k_d = jnp.where(inside[d], k_d, jnp.zeros_like(k_d))
                s_d = dot(k_d, q2, NT)
                if d == 0:
                    s_d = jnp.where(later, -jnp.inf, s_d)
                top = jnp.max(s_d, axis=0, keepdims=True)
                if d > 0:
                    top = jnp.where(inside[d], top, -jnp.inf)
                blocks.append(s_d)
                tops.append(top)
            top = functools.reduce(jnp.maximum, tops)
            exps = []
            norm = jnp.zeros_like(top)
            for d in range(SPAN):
                top_d = top if d == 0 else jnp.where(inside[d], top, jnp.inf)
                e_d = jnp.exp2((blocks[d] - top_d) * EXP2_SCALE)
                norm = norm + jnp.sum(e_d, axis=0, keepdims=True)
                exps.append(e_d)
            inv = 1.0 / norm
            delta = jnp.zeros_like(top)
            dps = []
            for d in range(SPAN):
                p_d = exps[d] * inv
                exps[d] = p_d
                p_s[d * ROWS : (d + 1) * ROWS, lo : lo + 2 * HD] = p_d.astype(jnp.bfloat16)
                dp_d = dot(kv[g, 1, d * ROWS : (d + 1) * ROWS], do2, NT)
                delta = delta + jnp.sum(p_d * dp_d, axis=0, keepdims=True)
                dps.append(dp_d)
            for d in range(SPAN):
                ds_d = exps[d] * (dps[d] - delta)
                ds_s[d * ROWS : (d + 1) * ROWS, lo : lo + 2 * HD] = ds_d.astype(jnp.bfloat16)
        q6 = jnp.concatenate([q_v[g, :, j * HD : (j + 1) * HD] for j in range(PER)], 0)
        do6 = jnp.concatenate([do_v[g, :, j * HD : (j + 1) * HD] for j in range(PER)], 0)
        dk = dot(ds_s[...], q6, NN) * INV_ROOT
        dv = dot(p_s[...], do6, NN)
        for w, d_w in enumerate((dk, dv)):
            own_terms[g, w] = d_w[0:ROWS]
            for d in range(1, SPAN):
                terms[g, d - 1, w] = d_w[d * ROWS : (d + 1) * ROWS].astype(jnp.bfloat16)

    def queries_out(g):
        dq_t = dot(k_t[...], ds_s[...], NN) * INV_ROOT
        for j in range(PER):
            dq_v[g, :, j * HD : (j + 1) * HD] = dq_t[:, j * HD : (j + 1) * HD].T.astype(jnp.bfloat16)

    def dq_store(g):
        return pltpu.make_async_copy(
            dq_v.at[g], dq_hbm.at[:, pl.ds(pl.multiple_of(g * WIDE, WIDE), WIDE)], store_sem.at[g]
        )

    send_own(0)
    send_own(1)
    relay(0)
    send_own(2)

    def step(g, carry):
        @pl.when(g < KVH - 1)
        def _():
            relay(g + 1)

            @pl.when(g < 1)
            def _():
                send_own(g + 3)

        wait_slot(g, 2)
        wait_slot(g, cross_slot)
        compute(g)
        send_far(g).start()
        send_near(g).start()
        queries_out(g)
        dq_store(g).start()

        @pl.when(g > 0)
        def _():
            reduce(g - 1)

        return carry

    lax.fori_loop(0, KVH, step, 0)
    for g in range(KVH - 1):
        finish(g)
    reduce(KVH - 1)
    finish(KVH - 1)
    for g in range(KVH):
        dk_out[:, g * HD : (g + 1) * HD] = own_terms[g, 0].astype(jnp.bfloat16)
        dv_out[:, g * HD : (g + 1) * HD] = own_terms[g, 1].astype(jnp.bfloat16)
    for g in range(KVH):
        own_cross(g).wait_send()
        relay_sibling(g).wait_send()
        send_near(g).wait_send()
        send_far(g).wait_send()
        send_sum(g).wait_send()
        dq_store(g).wait()

    @pl.when(is_even)
    def _():
        for g in range(KVH):
            own_sibling(g).wait_send()
            relay_cross(g).wait_send()


def solution(mesh):
    n_ctx = mesh.shape["ctx"]
    any_space = pl.BlockSpec(memory_space=pl.ANY)
    vmem = pl.BlockSpec(memory_space=pltpu.VMEM)
    bf16, f32 = jnp.bfloat16, jnp.float32

    def per_device(queries, key_vectors, value_vectors, d_output, doc_blocks):
        return pl.pallas_call(
            functools.partial(kernel, n_ctx),
            out_shape=(
                jax.ShapeDtypeStruct((ROWS, QH * HD), bf16),
                jax.ShapeDtypeStruct((ROWS, KVH * HD), bf16),
                jax.ShapeDtypeStruct((ROWS, KVH * HD), bf16),
            ),
            in_specs=[pl.BlockSpec(memory_space=pltpu.SMEM)] + [any_space] * 4,
            out_specs=(any_space, vmem, vmem),
            scratch_shapes=[
                pltpu.VMEM((KVH, ROWS, WIDE), bf16),
                pltpu.VMEM((KVH, ROWS, WIDE), bf16),
                pltpu.VMEM((KVH, ROWS, WIDE), bf16),
                pltpu.VMEM((KVH, 2, KEYS, HD), bf16),
                pltpu.VMEM((HD, KEYS), bf16),
                pltpu.VMEM((KEYS, WIDE), bf16),
                pltpu.VMEM((KEYS, WIDE), bf16),
                pltpu.VMEM((KVH, SPAN - 1, 2, ROWS, HD), bf16),
                pltpu.VMEM((KVH, 2, ROWS, HD), f32),
                pltpu.VMEM((KVH, 2, ROWS, HD), bf16),
                pltpu.VMEM((4, KVH, 2, ROWS, HD), bf16),
                pltpu.SemaphoreType.DMA((KVH, 2)),
                pltpu.SemaphoreType.DMA((KVH, 2)),
                pltpu.SemaphoreType.DMA((KVH,)),
                pltpu.SemaphoreType.DMA((4, KVH)),
                pltpu.SemaphoreType.DMA((SPAN, KVH)),
                pltpu.SemaphoreType.DMA((3, KVH)),
                pltpu.SemaphoreType.DMA((4, KVH)),
            ],
            compiler_params=pltpu.CompilerParams(
                collective_id=0, has_side_effects=True, vmem_limit_bytes=48 * 1024 * 1024
            ),
        )(doc_blocks, queries, key_vectors, value_vectors, d_output)

    spec = P(("dp", "ctx"), None)
    return jax.shard_map(
        per_device,
        mesh=mesh,
        in_specs=(spec, spec, spec, spec, P("dp")),
        out_specs=(spec, spec, spec),
        check_vma=False,
    )
```

time: 108 us -> 43.4 us (0.40)
  the two profiles are of different devices: /device:TPU:198 before, /device:TPU:1 now
where the time goes in v1:
time: 43.4 us; the launch traced here: 43.1 us
  Pallas kernels  35.6 us (82%)
  local copies, waits for them, and re-layouts  6.91 us (16%)
  between operations  0.65 us (1%)
    pallas_call x1, Pallas kernels, per_device(): pl.pallas_call(functools.partial(kernel, n_ctx), out_shape=(jax.ShapeDtyp...  35.6 us
    unnamed x13, local copies, waits for them, and re-layouts  6.91 us

profile of v1, /device:TPU:1, one launch (start us, length us, event | category | flops | bytes accessed | tf_op | source)
XLA Modules:
  0.0 43.1 jit_solution(10955916211182647925)
XLA Ops:
  0.6 0.0 copy-start
  0.6 1.1 %copy-done = bf16[128,3072]{1,0:T(8,128)(2,1)S(1)} copy-done((bf16[128,3072]{1,0:T(8,128)(2,1)S(1)}, bf16[128,3072]{1,0:T(8,128)(2,1)}, u32[]{:S(2)}) %copy-start) | copy-done | bytes 786456
  1.8 0.0 copy-start.1
  1.8 1.1 %copy-done.1 = bf16[128,3072]{1,0:T(8,128)(2,1)S(1)} copy-done((bf16[128,3072]{1,0:T(8,128)(2,1)S(1)}, bf16[128,3072]{1,0:T(8,128)(2,1)}, u32[]{:S(2)}) %copy-start.1) | copy-done | bytes 786456
  2.9 0.0 copy-start.2
  2.9 0.9 %copy-done.2 = bf16[128,512]{1,0:T(8,128)(2,1)S(1)} copy-done((bf16[128,512]{1,0:T(8,128)(2,1)S(1)}, bf16[128,512]{1,0:T(8,128)(2,1)}, u32[]{:S(2)}) %copy-start.2) | copy-done | bytes 131096
  3.8 0.0 copy-start.3
  3.8 0.9 %copy-done.3 = bf16[128,512]{1,0:T(8,128)(2,1)S(1)} copy-done((bf16[128,512]{1,0:T(8,128)(2,1)S(1)}, bf16[128,512]{1,0:T(8,128)(2,1)}, u32[]{:S(2)}) %copy-start.3) | copy-done | bytes 131096
  4.7 0.0 copy-start.4
  4.7 0.7 %copy-done.4 = s32[16]{0:T(128)S(1)} copy-done((s32[16]{0:T(128)S(1)}, s32[16]{0:T(128)}, u32[]{:S(2)}) %copy-start.4) | copy-done | bytes 88
  5.4 35.6 %shard_map.76 = (bf16[128,3072]{1,0:T(8,128)(2,1)S(1)}, bf16[128,512]{1,0:T(8,128)(2,1)S(1)}, bf16[128,512]{1,0:T(8,128)(2,1)S(1)}) custom-call(s32[16]{0:T(128)S(1)} %copy-done.4, bf16[128,3072]{1,0:T(8,128)(2,1)S(1)} %copy-done, bf16[128,512]{1,0:T(8,128)(2,1)S(1)} %copy-done.2, bf16[128,512]{1,0:T(8,128)(2,1)S(1)} %copy-done.3, ...), custom_call_target="tpu_custom_call" | custom-call | tf_op jit(solution)/shard_map/pallas_call | solution.py:351
  40.9 0.9 %copy.11 = bf16[128,3072]{1,0:T(8,128)(2,1)} copy(bf16[128,3072]{1,0:T(8,128)(2,1)S(1)} %get-tuple-element.6) | data formatting | bytes 1572864
  41.8 0.7 %copy.12 = bf16[128,512]{1,0:T(8,128)(2,1)} copy(bf16[128,512]{1,0:T(8,128)(2,1)S(1)} %get-tuple-element.7) | data formatting | bytes 262144
  42.5 0.7 %copy.13 = bf16[128,512]{1,0:T(8,128)(2,1)} copy(bf16[128,512]{1,0:T(8,128)(2,1)S(1)} %get-tuple-element.8) | data formatting | bytes 262144
Async XLA Ops:
  0.6 1.1 %copy-start = (bf16[128,3072]{1,0:T(8,128)(2,1)S(1)}, bf16[128,3072]{1,0:T(8,128)(2,1)}, u32[]{:S(2)}) copy-start(bf16[128,3072]{1,0:T(8,128)(2,1)} %q_hbm.1) | copy-start | bytes 2359300
  1.8 1.1 %copy-start.1 = (bf16[128,3072]{1,0:T(8,128)(2,1)S(1)}, bf16[128,3072]{1,0:T(8,128)(2,1)}, u32[]{:S(2)}) copy-start(bf16[128,3072]{1,0:T(8,128)(2,1)} %do_hbm.1) | copy-start | bytes 2359300
  2.9 0.9 %copy-start.2 = (bf16[128,512]{1,0:T(8,128)(2,1)S(1)}, bf16[128,512]{1,0:T(8,128)(2,1)}, u32[]{:S(2)}) copy-start(bf16[128,512]{1,0:T(8,128)(2,1)} %k_hbm.1) | copy-start | bytes 393220
  3.8 0.9 %copy-start.3 = (bf16[128,512]{1,0:T(8,128)(2,1)S(1)}, bf16[128,512]{1,0:T(8,128)(2,1)}, u32[]{:S(2)}) copy-start(bf16[128,512]{1,0:T(8,128)(2,1)} %v_hbm.1) | copy-start | bytes 393220
  4.7 0.7 %copy-start.4 = (s32[16]{0:T(128)S(1)}, s32[16]{0:T(128)}, u32[]{:S(2)}) copy-start(s32[16]{0:T(128)} %docs.1) | copy-start | bytes 196

commit v2 on v1

v2 whole, which is shorter than its diff:
```python
import functools
import math

import jax
import jax.numpy as jnp
from jax import lax
from jax.experimental import pallas as pl
from jax.experimental.pallas import tpu as pltpu
from jax.sharding import PartitionSpec as P

QH = 24
KVH = 4
HD = 128
PER = QH // KVH
ROWS = 128
SPAN = 4
NDOCS = 16
WIDE = PER * HD
PAIRS = PER // 2
INV_ROOT = 1.0 / math.sqrt(HD)
EXP2_SCALE = INV_ROOT * math.log2(math.e)
MESH = pl.DeviceIdType.MESH
NT = (((1,), (1,)), ((), ()))
NN = (((1,), (0,)), ((), ()))
KEYS = SPAN * ROWS
STORES = 4


def dot(a, b, dims):
    return lax.dot_general(a, b, dims, preferred_element_type=jnp.float32)


def kernel(
    n_ctx,
    docs_hbm,
    q_hbm,
    k_hbm,
    v_hbm,
    do_hbm,
    dq_out,
    dk_out,
    dv_out,
    docs,
    q_v,
    do_v,
    kv,
    k_t,
    p_s,
    ds_s,
    terms,
    own_terms,
    sums,
    back,
    docs_sem,
    load_sem,
    kv_sem,
    send_sem,
    recv_sem,
    back_send,
    back_recv,
):
    me = lax.axis_index("ctx")
    core = lax.rem(me, 2)
    chip = lax.div(me, 2)
    sibling = chip * 2 + (1 - core)
    near_slot = 1 + 2 * core
    far = 3 - 2 * core

    is_even, is_odd = core == 0, core == 1
    before, after = chip >= 1, me + 2 < n_ctx
    even_before, odd_before = is_even & before, is_odd & before
    even_after, odd_after = is_even & after, is_odd & after
    relays_on = even_before & after
    straight_from, straight_to = is_even & (chip >= 2), is_odd & (me + 3 < n_ctx)

    barrier = pltpu.get_barrier_semaphore()
    partners = (
        (me >= 0, sibling),
        (even_before, me - 1),
        (odd_after, me + 1),
        (even_after, me + 3),
        (odd_before, me - 3),
        (even_after, me + 2),
        (even_before, me - 2),
        (straight_from, me - 3),
        (straight_to, me + 3),
    )
    for there, device in partners:

        @pl.when(there)
        def _():
            pl.semaphore_signal(barrier, inc=1, device_id={"ctx": device}, device_id_type=MESH)

    docs_copy = pltpu.make_async_copy(docs_hbm, docs, docs_sem)
    docs_copy.start()

    def kv_load(g, which):
        src = (k_hbm, v_hbm)[which]
        return pltpu.make_async_copy(
            src.at[:, g * HD : (g + 1) * HD], kv.at[g, which, 0:ROWS], kv_sem.at[g, which]
        )

    for g in range(KVH):
        for which in range(2):
            kv_load(g, which).start()

    def q_load(g):
        cols = slice(g * WIDE, (g + 1) * WIDE)
        return (
            pltpu.make_async_copy(q_hbm.at[:, cols], q_v.at[g], load_sem.at[g, 0]),
            pltpu.make_async_copy(do_hbm.at[:, cols], do_v.at[g], load_sem.at[g, 1]),
        )

    for g in range(KVH):
        for copy in q_load(g):
            copy.start()

    @pl.when(me < SPAN - 1)
    def _():
        for d in range(1, SPAN):

            @pl.when(me < d)
            def _():
                kv[:, :, d * ROWS : (d + 1) * ROWS] = jnp.zeros((KVH, 2, ROWS, HD), jnp.bfloat16)

    for g in range(KVH):
        for which in range(2):
            kv_load(g, which).wait()
    docs_copy.wait()

    end = jnp.int32(0)
    start = jnp.int32(0)
    for i in range(NDOCS):
        end = end + docs[i]
        start = jnp.where(end <= me, end, start)
    inside = [me - d >= start for d in range(SPAN)]

    pl.semaphore_wait(barrier, sum(there.astype(jnp.int32) for there, _ in partners))

    def kv_copy(g, from_slot, to_slot, kind, device):
        return pltpu.make_async_remote_copy(
            src_ref=kv.at[g, :, pl.ds(pl.multiple_of(from_slot * ROWS, ROWS), ROWS)],
            dst_ref=kv.at[g, :, pl.ds(pl.multiple_of(to_slot * ROWS, ROWS), ROWS)],
            send_sem=send_sem.at[kind, g],
            recv_sem=recv_sem.at[to_slot, g],
            device_id={"ctx": device},
            device_id_type=MESH,
        )

    def own_cross(g):
        return kv_copy(g, 0, far, 0, me + far)

    def own_sibling(g):
        return kv_copy(g, 0, 1, 1, sibling)

    def pass_sibling(g):
        return kv_copy(g, near_slot, 2, 2, sibling)

    def pass_cross(g):
        return kv_copy(g, 1, 3, 3, me + 2)

    def send_cross(g):
        @pl.when(after)
        def _():
            own_cross(g).start()

    def send_sibling(g):
        @pl.when(is_even)
        def _():
            own_sibling(g).start()

    def wait_slot(g, slot, there):
        @pl.when(there)
        def _():
            kv_copy(g, 0, slot, 0, sibling).wait_recv()

    def relay(g):
        @pl.when(before)
        def _():
            kv_copy(g, 0, near_slot, 0, sibling).wait_recv()

            pass_sibling(g).start()

            @pl.when(relays_on)
            def _():
                pass_cross(g).start()

    def wait_keys(g):
        wait_slot(g, 2, before)
        wait_slot(g, far, is_odd | (chip >= 2))

    def back_copy(src, slot, kind, g, device):
        return pltpu.make_async_remote_copy(
            src_ref=src,
            dst_ref=back.at[slot, g],
            send_sem=back_send.at[kind, g],
            recv_sem=back_recv.at[slot, g],
            device_id={"ctx": device},
            device_id_type=MESH,
        )

    far_on = is_odd | (chip >= 2)

    early_sum = is_odd | jnp.logical_not(straight_from & after)

    def by_chip(g):
        return (g < KVH - 1) & (is_even & (me != 4))

    def joins(g):
        return (g < KVH - 1) & (straight_from & after)

    def send_pair(g):
        return back_copy(terms.at[g, 1], 0, 0, g, sibling)

    def send_far(g):
        slot = jnp.where(by_chip(g), 3, 2)
        device = jnp.where(by_chip(g), me - 2, me - far)
        return back_copy(terms.at[g, far - 1], slot, 1, g, device)

    def send_sum(g):
        return back_copy(sums.at[g], 1, 2, g, me - near_slot)

    def wait_back(slot, g):
        back_copy(sums.at[g], slot, 2, g, sibling).wait_recv()

    def reduce(g):
        @pl.when(before)
        def _():
            wait_back(0, g)

            @pl.when(joins(g))
            def _():
                wait_back(3, g)
                for w in range(2):
                    total = terms[g, 0, w].astype(jnp.float32) + back[0, g, w].astype(jnp.float32)
                    sums[g, w] = (total + back[3, g, w].astype(jnp.float32)).astype(jnp.bfloat16)

            @pl.when(jnp.logical_not(joins(g)))
            def _():
                for w in range(2):
                    mine = terms[g, near_slot - 1, w].astype(jnp.float32)
                    sums[g, w] = (mine + back[0, g, w].astype(jnp.float32)).astype(jnp.bfloat16)

            send_sum(g).start()

    def finish(g):
        @pl.when(is_even | (straight_to & (me == 1 if g < KVH - 1 else me >= 0)))
        def _():
            wait_back(2, g)
            for w in range(2):
                own_terms[g, w] += back[2, g, w].astype(jnp.float32)

        @pl.when(after)
        def _():
            wait_back(1, g)
            for w in range(2):
                own_terms[g, w] += back[1, g, w].astype(jnp.float32)

    later = lax.broadcasted_iota(jnp.int32, (ROWS, 2 * ROWS), 0) > lax.rem(
        lax.broadcasted_iota(jnp.int32, (ROWS, 2 * ROWS), 1), ROWS
    )

    def between(g):
        @pl.when(g < KVH - 2)
        def _():
            relay(g + 2)

        @pl.when((g > 0) & early_sum)
        def _():
            reduce(g - 1)

    def compute(g):
        for which in range(2):
            pltpu.make_async_copy(
                (q_v, do_v)[which].at[g], (q_v, do_v)[which].at[g], load_sem.at[g, which]
            ).wait()
        keys = kv[g, 0]
        k_t[...] = keys.T
        for pair in range(PAIRS):
            lo = pair * 2 * HD
            q2 = jnp.concatenate([q_v[g, :, lo : lo + HD], q_v[g, :, lo + HD : lo + 2 * HD]], 0)
            do2 = jnp.concatenate([do_v[g, :, lo : lo + HD], do_v[g, :, lo + HD : lo + 2 * HD]], 0)
            blocks = []
            tops = []
            for d in range(SPAN):
                k_d = kv[g, 0, d * ROWS : (d + 1) * ROWS]
                if d > 0:
                    k_d = jnp.where(inside[d], k_d, jnp.zeros_like(k_d))
                s_d = dot(k_d, q2, NT)
                if d == 0:
                    s_d = jnp.where(later, -jnp.inf, s_d)
                top = jnp.max(s_d, axis=0, keepdims=True)
                if d > 0:
                    top = jnp.where(inside[d], top, -jnp.inf)
                blocks.append(s_d)
                tops.append(top)
            top = functools.reduce(jnp.maximum, tops)
            exps = []
            norm = jnp.zeros_like(top)
            for d in range(SPAN):
                top_d = top if d == 0 else jnp.where(inside[d], top, jnp.inf)
                e_d = jnp.exp2((blocks[d] - top_d) * EXP2_SCALE)
                norm = norm + jnp.sum(e_d, axis=0, keepdims=True)
                exps.append(e_d)
            inv = 1.0 / norm
            delta = jnp.zeros_like(top)
            dps = []
            for d in range(SPAN):
                p_d = exps[d] * inv
                exps[d] = p_d
                p_s[d * ROWS : (d + 1) * ROWS, lo : lo + 2 * HD] = p_d.astype(jnp.bfloat16)
                dp_d = dot(kv[g, 1, d * ROWS : (d + 1) * ROWS], do2, NT)
                delta = delta + jnp.sum(p_d * dp_d, axis=0, keepdims=True)
                dps.append(dp_d)
            for d in range(SPAN):
                ds_d = exps[d] * (dps[d] - delta)
                ds_s[d * ROWS : (d + 1) * ROWS, lo : lo + 2 * HD] = ds_d.astype(jnp.bfloat16)
        between(g)
        q6 = jnp.concatenate([q_v[g, :, j * HD : (j + 1) * HD] for j in range(PER)], 0)
        do6 = jnp.concatenate([do_v[g, :, j * HD : (j + 1) * HD] for j in range(PER)], 0)
        half = 2 * ROWS
        dk = dot(ds_s[half:], q6, NN) * INV_ROOT
        dv = dot(p_s[half:], do6, NN)
        for w, d_w in enumerate((dk, dv)):
            for d in range(2):
                terms[g, d + 1, w] = d_w[d * ROWS : (d + 1) * ROWS].astype(jnp.bfloat16)

        @pl.when(before)
        def _():
            send_pair(g).start()

        @pl.when(straight_from)
        def _():
            send_far(g).start()

        dk = dot(ds_s[:half], q6, NN) * INV_ROOT
        dv = dot(p_s[:half], do6, NN)
        for w, d_w in enumerate((dk, dv)):
            own_terms[g, w] = d_w[0:ROWS]
            terms[g, 0, w] = d_w[ROWS:half].astype(jnp.bfloat16)

        @pl.when(is_odd)
        def _():
            send_far(g).start()

    def queries_out(g):
        dq_t = dot(k_t[...], ds_s[...], NN) * INV_ROOT
        for j in range(PER):
            col = pl.multiple_of(g * WIDE + j * HD, HD)
            dq_out[:, pl.ds(col, HD)] = dq_t[:, j * HD : (j + 1) * HD].T.astype(jnp.bfloat16)

    send_cross(0)
    send_sibling(0)
    send_cross(1)
    for g in range(1, KVH):
        send_sibling(g)
    for g in range(2):
        relay(g)
        send_cross(g + 2)

    def step(g, carry):
        wait_keys(g)
        compute(g)
        queries_out(g)

        @pl.when((g > 1) & jnp.logical_not(early_sum))
        def _():
            reduce(g - 2)

        return carry

    lax.fori_loop(0, KVH, step, 0)

    @pl.when(jnp.logical_not(early_sum))
    def _():
        reduce(KVH - 2)

    reduce(KVH - 1)
    for g in range(KVH):
        finish(g)
        dk_out[:, g * HD : (g + 1) * HD] = own_terms[g, 0].astype(jnp.bfloat16)
        dv_out[:, g * HD : (g + 1) * HD] = own_terms[g, 1].astype(jnp.bfloat16)

    def drain(there, copies):
        @pl.when(there)
        def _():
            for copy in copies:
                copy.wait_send()

    drain(after, [own_cross(g) for g in range(KVH)])
    drain(is_even, [own_sibling(g) for g in range(KVH)])
    drain(relays_on, [pass_cross(g) for g in range(KVH)])
    drain(far_on, [send_far(g) for g in range(KVH)])
    drain(before, [c(g) for g in range(KVH) for c in (pass_sibling, send_pair, send_sum)])


def store_kernel(dq, dk, dv, dq_out, dk_out, dv_out, sems):
    part = ROWS // STORES
    slices = [slice(i * part, (i + 1) * part) for i in range(STORES)]
    pairs = [(dq.at[rows], dq_out.at[rows]) for rows in slices] + [(dk, dk_out), (dv, dv_out)]
    copies = [pltpu.make_async_copy(src, dst, sems.at[i]) for i, (src, dst) in enumerate(pairs)]
    for copy in copies:
        copy.start()
    for copy in copies:
        copy.wait()


def solution(mesh):
    n_ctx = mesh.shape["ctx"]
    hbm = pl.BlockSpec(memory_space=pltpu.HBM)
    vmem = pl.BlockSpec(memory_space=pltpu.VMEM)
    bf16, f32 = jnp.bfloat16, jnp.float32

    def per_device(queries, key_vectors, value_vectors, d_output, doc_blocks):
        results = pl.pallas_call(
            functools.partial(kernel, n_ctx),
            out_shape=(
                jax.ShapeDtypeStruct((ROWS, QH * HD), bf16),
                jax.ShapeDtypeStruct((ROWS, KVH * HD), bf16),
                jax.ShapeDtypeStruct((ROWS, KVH * HD), bf16),
            ),
            in_specs=[hbm] * 5,
            out_specs=(vmem, vmem, vmem),
            scratch_shapes=[
                pltpu.SMEM((NDOCS,), jnp.int32),
                pltpu.VMEM((KVH, ROWS, WIDE), bf16),
                pltpu.VMEM((KVH, ROWS, WIDE), bf16),
                pltpu.VMEM((KVH, 2, KEYS, HD), bf16),
                pltpu.VMEM((HD, KEYS), bf16),
                pltpu.VMEM((KEYS, WIDE), bf16),
                pltpu.VMEM((KEYS, WIDE), bf16),
                pltpu.VMEM((KVH, SPAN - 1, 2, ROWS, HD), bf16),
                pltpu.VMEM((KVH, 2, ROWS, HD), f32),
                pltpu.VMEM((KVH, 2, ROWS, HD), bf16),
                pltpu.VMEM((4, KVH, 2, ROWS, HD), bf16),
                pltpu.SemaphoreType.DMA,
                pltpu.SemaphoreType.DMA((KVH, 2)),
                pltpu.SemaphoreType.DMA((KVH, 2)),
                pltpu.SemaphoreType.DMA((4, KVH)),
                pltpu.SemaphoreType.DMA((SPAN, KVH)),
                pltpu.SemaphoreType.DMA((3, KVH)),
                pltpu.SemaphoreType.DMA((4, KVH)),
            ],
            compiler_params=pltpu.CompilerParams(
                collective_id=0, has_side_effects=True, vmem_limit_bytes=40 * 1024 * 1024
            ),
        )(
            *(
                pltpu.with_memory_space_constraint(x, pltpu.HBM)
                for x in (doc_blocks, queries, key_vectors, value_vectors, d_output)
            )
        )
        return pl.pallas_call(
            store_kernel,
            out_shape=[jax.ShapeDtypeStruct(x.shape, x.dtype) for x in results],
            in_specs=[vmem] * 3,
            out_specs=[hbm] * 3,
            scratch_shapes=[pltpu.SemaphoreType.DMA((STORES + 2,))],
        )(*(pltpu.with_memory_space_constraint(x, pltpu.VMEM) for x in results))

    spec = P(("dp", "ctx"), None)
    return jax.shard_map(
        per_device,
        mesh=mesh,
        in_specs=(spec, spec, spec, spec, P("dp")),
        out_specs=(spec, spec, spec),
        check_vma=False,
    )
```

time: 43.4 us -> 30.4 us (0.70)
  local copies, waits for them, and re-layouts: 6.91 us -> 0 us
  Pallas kernels: 35.6 us -> 29.3 us
    pallas_call x1, Pallas kernels: 35.6 us -> 28.3 us  [per_device(): pl.pallas_call(functools.partial(kernel, n_ctx), out_shape=(jax.ShapeDtyp...]
    unnamed x13 -> x0, local copies, waits for them, and re-layouts: 6.91 us -> none
    pallas_call x0 -> x1, Pallas kernels: none -> 1.01 us  [per_device(): pl.pallas_call(store_kernel, out_shape=[jax.ShapeDtypeStruct(x.shape, x.d...]
where the time goes in v2:
time: 30.4 us; the launch traced here: 29.9 us
  Pallas kernels  29.3 us (96%)
  between operations  0.64 us (2%)
    pallas_call x1, Pallas kernels, per_device(): pl.pallas_call(functools.partial(kernel, n_ctx), out_shape=(jax.ShapeDtyp...  28.3 us
    pallas_call x1, Pallas kernels, per_device(): pl.pallas_call(store_kernel, out_shape=[jax.ShapeDtypeStruct(x.shape, x.d...  1.01 us

profile of v2, /device:TPU:1, one launch (start us, length us, event | category | flops | bytes accessed | tf_op | source)
XLA Modules:
  0.0 29.9 jit_solution(14515050118351760979)
XLA Ops:
  0.6 28.3 %shard_map.76 = (bf16[128,3072]{1,0:T(8,128)(2,1)S(1)}, bf16[128,512]{1,0:T(8,128)(2,1)S(1)}, bf16[128,512]{1,0:T(8,128)(2,1)S(1)}) custom-call(s32[16]{0:T(128)} %docs_hbm.1, bf16[128,3072]{1,0:T(8,128)(2,1)} %q_hbm.1, bf16[128,512]{1,0:T(8,128)(2,1)} %k_hbm.1, bf16[128,512]{1,0:T(8,128)(2,1)} %v_hbm.1, bf16[128,3072]{1,0:T(8,128)(2,1)} %do_hbm.1), custom_call_target="tpu_custom_call" | custom-call | tf_op jit(solution)/shard_map/pallas_call | solution.py:415
  28.9 1.0 %shard_map.77 = (bf16[128,3072]{1,0:T(8,128)(2,1)}, bf16[128,512]{1,0:T(8,128)(2,1)}, bf16[128,512]{1,0:T(8,128)(2,1)}) custom-call(bf16[128,3072]{1,0:T(8,128)(2,1)S(1)} %get-tuple-element.6.dq, bf16[128,512]{1,0:T(8,128)(2,1)S(1)} %get-tuple-element.7.dk, bf16[128,512]{1,0:T(8,128)(2,1)S(1)} %get-tuple-element.8.dv), custom_call_target="tpu_custom_call" | custom-call | tf_op jit(solution)/shard_map/pallas_call | solution.py:453

commit v3 on v2

--- a/solution.py
+++ b/solution.py
@@ -23,7 +23,6 @@
 NT = (((1,), (1,)), ((), ()))
 NN = (((1,), (0,)), ((), ()))
 KEYS = SPAN * ROWS
-STORES = 4
 
 
 def dot(a, b, dims):
@@ -260,11 +259,12 @@
         lax.broadcasted_iota(jnp.int32, (ROWS, 2 * ROWS), 1), ROWS
     )
 
+    def relay_ahead(g):
+        @pl.when(g < KVH - 2)
+        def _():
+            relay(g + 2)
+
     def between(g):
-        @pl.when(g < KVH - 2)
-        def _():
-            relay(g + 2)
-
         @pl.when((g > 0) & early_sum)
         def _():
             reduce(g - 1)
@@ -277,6 +277,8 @@
         keys = kv[g, 0]
         k_t[...] = keys.T
         for pair in range(PAIRS):
+            if pair == 1:
+                relay_ahead(g)
             lo = pair * 2 * HD
             q2 = jnp.concatenate([q_v[g, :, lo : lo + HD], q_v[g, :, lo + HD : lo + 2 * HD]], 0)
             do2 = jnp.concatenate([do_v[g, :, lo : lo + HD], do_v[g, :, lo + HD : lo + 2 * HD]], 0)
@@ -395,10 +397,10 @@
 
 
 def store_kernel(dq, dk, dv, dq_out, dk_out, dv_out, sems):
-    part = ROWS // STORES
-    slices = [slice(i * part, (i + 1) * part) for i in range(STORES)]
-    pairs = [(dq.at[rows], dq_out.at[rows]) for rows in slices] + [(dk, dk_out), (dv, dv_out)]
-    copies = [pltpu.make_async_copy(src, dst, sems.at[i]) for i, (src, dst) in enumerate(pairs)]
+    copies = [
+        pltpu.make_async_copy(src, dst, sems.at[i])
+        for i, (src, dst) in enumerate(((dq, dq_out), (dk, dk_out), (dv, dv_out)))
+    ]
     for copy in copies:
         copy.start()
     for copy in copies:
@@ -455,7 +457,7 @@
             out_shape=[jax.ShapeDtypeStruct(x.shape, x.dtype) for x in results],
             in_specs=[vmem] * 3,
             out_specs=[hbm] * 3,
-            scratch_shapes=[pltpu.SemaphoreType.DMA((STORES + 2,))],
+            scratch_shapes=[pltpu.SemaphoreType.DMA((3,))],
         )(*(pltpu.with_memory_space_constraint(x, pltpu.VMEM) for x in results))
 
     spec = P(("dp", "ctx"), None)

time: 30.4 us -> 31.5 us (1.036)
  Pallas kernels: 29.3 us -> 30.5 us
    pallas_call x1, Pallas kernels: 28.3 us -> 29.5 us  [per_device(): pl.pallas_call(functools.partial(kernel, n_ctx), out_shape=(jax.ShapeDtyp...]
where the time goes in v3:
time: 31.5 us; the launch traced here: 31.1 us
  Pallas kernels  30.5 us (97%)
  between operations  0.64 us (2%)
    pallas_call x1, Pallas kernels, per_device(): pl.pallas_call(functools.partial(kernel, n_ctx), out_shape=(jax.ShapeDtyp...  29.5 us
    pallas_call x1, Pallas kernels, per_device(): pl.pallas_call(store_kernel, out_shape=[jax.ShapeDtypeStruct(x.shape, x.d...  0.99 us

profile of v3, /device:TPU:1, one launch (start us, length us, event | category | flops | bytes accessed | tf_op | source)
XLA Modules:
  0.0 31.1 jit_solution(11757308226183509281)
XLA Ops:
  0.6 29.5 %shard_map.76 = (bf16[128,3072]{1,0:T(8,128)(2,1)S(1)}, bf16[128,512]{1,0:T(8,128)(2,1)S(1)}, bf16[128,512]{1,0:T(8,128)(2,1)S(1)}) custom-call(s32[16]{0:T(128)} %docs_hbm.1, bf16[128,3072]{1,0:T(8,128)(2,1)} %q_hbm.1, bf16[128,512]{1,0:T(8,128)(2,1)} %k_hbm.1, bf16[128,512]{1,0:T(8,128)(2,1)} %v_hbm.1, bf16[128,3072]{1,0:T(8,128)(2,1)} %do_hbm.1), custom_call_target="tpu_custom_call" | custom-call | tf_op jit(solution)/shard_map/pallas_call | solution.py:417
  30.2 1.0 %shard_map.77 = (bf16[128,3072]{1,0:T(8,128)(2,1)}, bf16[128,512]{1,0:T(8,128)(2,1)}, bf16[128,512]{1,0:T(8,128)(2,1)}) custom-call(bf16[128,3072]{1,0:T(8,128)(2,1)S(1)} %get-tuple-element.6.dq, bf16[128,512]{1,0:T(8,128)(2,1)S(1)} %get-tuple-element.7.dk, bf16[128,512]{1,0:T(8,128)(2,1)S(1)} %get-tuple-element.8.dv), custom_call_target="tpu_custom_call" | custom-call | tf_op jit(solution)/shard_map/pallas_call | solution.py:455
